TPU v7x, 1024 devices: a whole 8x8x8 slice. The times are simulated.
1024 devices in a mesh: dp: 4 (over y_hi), fsdp: 256 (over x, y_lo, z, core).
Axes of the slice: x: 8, y: 8 (y_hi: 4, y_lo: 2; y = y_hi * 2 + y_lo), z: 8, core: 2. Of those that a mesh axis runs over, the one named last changes fastest.
Arguments:
- actor_gate: bfloat16 [27648, 1024], P('fsdp', 'dp'), may hold values from -6 to 6
- actor_up: bfloat16 [27648, 1024], P('fsdp', 'dp'), may hold values from -6 to 6
- actor_cotangent: bfloat16 [1024, 5120], P(('dp', 'fsdp')), may hold values from -3 to 3
- actor_down: bfloat16 [27648, 5120], P('fsdp'), may hold values from -0.078125 to 0.078125
- critic_gate: bfloat16 [27648, 1024], P('fsdp', 'dp'), may hold values from -6 to 6
- critic_up: bfloat16 [27648, 1024], P('fsdp', 'dp'), may hold values from -6 to 6
- critic_cotangent: bfloat16 [1024, 5120], P(('dp', 'fsdp')), may hold values from -3 to 3
- critic_down: bfloat16 [27648, 5120], P('fsdp'), may hold values from -0.078125 to 0.078125
Outputs:
- actor_down_grad: float32 [27648, 5120], P('fsdp', 'dp')
- actor_gate_grad: bfloat16 [27648, 1024], P('fsdp', 'dp')
- actor_up_grad: bfloat16 [27648, 1024], P('fsdp', 'dp')
- critic_down_grad: float32 [27648, 5120], P('fsdp', 'dp')
- critic_gate_grad: bfloat16 [27648, 1024], P('fsdp', 'dp')
- critic_up_grad: bfloat16 [27648, 1024], P('fsdp', 'dp')
All inputs are finite; a program needn't handle non-finite values.
Results may differ from a plain program's by a relative error of at most 0.012.
Values may be sent and summed in bfloat16 or wider, within the bound.
A program may use at most 64 MiB of HBM per device.

v0:
```python
import jax
import jax.numpy as jnp
from jax import lax
from jax.sharding import PartitionSpec as P


def activation(gate, up):
    gate32 = gate.astype(jnp.float32)
    up32 = up.astype(jnp.float32)
    sig = jax.nn.sigmoid(gate32)
    silu_val = gate32 * sig
    hidden = (silu_val * up32).astype(jnp.bfloat16)
    return (hidden, gate32, up32, sig, silu_val)


def input_grads(hidden_grad, gate32, up32, sig, silu_val):
    gate_grad = (hidden_grad * up32 * sig * (1.0 + gate32 * (1.0 - sig))).astype(jnp.bfloat16)
    up_grad = (hidden_grad * silu_val).astype(jnp.bfloat16)
    return (gate_grad, up_grad)


def back_project(down, rows):
    return lax.dot_general(down, rows, (((1,), (1,)), ((), ())), preferred_element_type=jnp.float32)


def on_device(
    actor_gate,
    actor_up,
    actor_cotangent,
    actor_down,
    critic_gate,
    critic_up,
    critic_cotangent,
    critic_down,
):
    actor_act = activation(actor_gate, actor_up)
    critic_act = activation(critic_gate, critic_up)
    actor_hidden = actor_act[0]
    critic_hidden = critic_act[0]
    actor_rows, critic_rows = (
        lax.all_gather(actor_cotangent, "fsdp", axis=0, tiled=True),
        lax.all_gather(critic_cotangent, "fsdp", axis=0, tiled=True),
    )
    actor_wpart = jnp.dot(actor_hidden, actor_rows, preferred_element_type=jnp.float32)
    critic_wpart = jnp.dot(critic_hidden, critic_rows, preferred_element_type=jnp.float32)
    actor_hgrad = back_project(actor_down, actor_rows)
    critic_hgrad = back_project(critic_down, critic_rows)
    actor_wpart = actor_wpart.astype(jnp.bfloat16).astype(jnp.float32)
    critic_wpart = critic_wpart.astype(jnp.bfloat16).astype(jnp.float32)
    actor_wgrad, critic_wgrad = (
        lax.psum_scatter(
            actor_wpart.astype(jnp.bfloat16), "dp", scatter_dimension=1, tiled=True
        ).astype(jnp.float32),
        lax.psum_scatter(
            critic_wpart.astype(jnp.bfloat16), "dp", scatter_dimension=1, tiled=True
        ).astype(jnp.float32),
    )
    actor_ggrad, actor_ugrad = input_grads(actor_hgrad, *actor_act[1:])
    critic_ggrad, critic_ugrad = input_grads(critic_hgrad, *critic_act[1:])
    return (actor_wgrad, actor_ggrad, actor_ugrad, critic_wgrad, critic_ggrad, critic_ugrad)


def solution(mesh):
    placed = (
        P("fsdp", "dp"),
        P("fsdp", "dp"),
        P(("dp", "fsdp"), None),
        P("fsdp", None),
        P("fsdp", "dp"),
        P("fsdp", "dp"),
        P(("dp", "fsdp"), None),
        P("fsdp", None),
    )
    return jax.shard_map(
        on_device,
        mesh=mesh,
        in_specs=placed,
        out_specs=(
            P("fsdp", "dp"),
            P("fsdp", "dp"),
            P("fsdp", "dp"),
            P("fsdp", "dp"),
            P("fsdp", "dp"),
            P("fsdp", "dp"),
        ),
        check_vma=False,
    )
```

profile of v0, /device:TPU:1, one launch (start us, length us, event | category | flops | bytes accessed | tf_op | source)
XLA Modules:
  0.0 968.3 jit_solution(3001962819079274976)
XLA Ops:
  7.2 0.0 copy-start
  7.2 0.0 copy-start.3
  7.2 0.0 copy-start.4
  7.2 0.0 all-gather.5.cloned.1.call-start
  7.2 0.7 all-gather.5.cloned.1.call-update
  7.9 0.0 all-gather.7.cloned.1.call-start
  8.0 0.7 all-gather.7.cloned.1.call-update
  8.7 0.0 reduce-scatter.3.cloned.1.call-start
  8.7 438.0 %all-gather.5.cloned.1.call-done = bf16[256,1,5120]{2,1,0:T(2,128)(2,1)} async-done(((bf16[1,1,5120]{2,1,0:T(2,128)(2,1)}), bf16[256,1,5120]{2,1,0:T(2,128)(2,1)}) %all-gather.5.cloned.1.call-update) | async-done | bytes 2621456 | tf_op jit(solution)/shard_map/all_gather | solution.py:41
  446.8 4.6 convolution_convert_fusion.1
  451.4 0.0 reduce-scatter.3.cloned.1.call-update
  451.4 0.0 copy-start.1
  451.4 0.0 copy-start.2
  451.4 0.0 reduce-scatter.5.cloned.1.call-start
  451.5 421.8 %all-gather.7.cloned.1.call-done = bf16[256,1,5120]{2,1,0:T(2,128)(2,1)} async-done(((bf16[1,1,5120]{2,1,0:T(2,128)(2,1)}), bf16[256,1,5120]{2,1,0:T(2,128)(2,1)}) %all-gather.7.cloned.1.call-update) | async-done | bytes 2621456 | tf_op jit(solution)/shard_map/all_gather | solution.py:42
  873.3 4.6 convolution_convert_fusion
  877.8 0.0 reduce-scatter.5.cloned.1.call-update
  877.9 0.0 copy-start.5
  877.9 4.3 multiply_convert_fusion.1
  882.2 4.2 multiply_convert_fusion
  886.4 31.0 %reduce-scatter.3.cloned.1.call-done = bf16[108,1280]{1,0:T(8,128)(2,1)} async-done(((bf16[108,5120]{1,0:T(8,128)(2,1)}), bf16[108,1280]{1,0:T(8,128)(2,1)}) %reduce-scatter.3.cloned.1.call-update) | async-done | bytes 276496 | tf_op jit(solution)/shard_map/reduce_scatter | solution.py:51
  917.4 1.8 convert_element_type.50
  919.2 40.8 %reduce-scatter.5.cloned.1.call-done = bf16[108,1280]{1,0:T(8,128)(2,1)} async-done(((bf16[108,5120]{1,0:T(8,128)(2,1)}), bf16[108,1280]{1,0:T(8,128)(2,1)}) %reduce-scatter.5.cloned.1.call-update) | async-done | bytes 276496 | tf_op jit(solution)/shard_map/reduce_scatter | solution.py:54
  960.0 1.8 convert_element_type.57
  (6 shorter events, 0.0 us)
Async XLA Ops:
  7.2 870.7 %copy-start = (bf16[108,5120]{1,0:T(8,128)(2,1)S(1)}, bf16[108,5120]{1,0:T(8,128)(2,1)}, u32[]{:S(2)}) copy-start(bf16[108,5120]{1,0:T(8,128)(2,1)} %param.11) | copy-start | bytes 3317764
  7.2 866.1 %copy-start.3 = (bf16[108,256]{1,0:T(8,128)(2,1)S(1)}, bf16[108,256]{1,0:T(8,128)(2,1)}, u32[]{:S(2)}) copy-start(bf16[108,256]{1,0:T(8,128)(2,1)} %param.13) | copy-start | bytes 165892
  7.2 866.1 %copy-start.4 = (bf16[108,256]{1,0:T(8,128)(2,1)S(1)}, bf16[108,256]{1,0:T(8,128)(2,1)}, u32[]{:S(2)}) copy-start(bf16[108,256]{1,0:T(8,128)(2,1)} %param.12) | copy-start | bytes 165892
  7.2 439.6 %all-gather.5.cloned.1.call-start = ((), (), s32[]{:S(2)}) async-start(), calls=%async_computation.4 | async-start | bytes 5263360 | tf_op jit(solution)/shard_map/all_gather | solution.py:41
  7.9 865.3 %all-gather.7.cloned.1.call-start = ((), (), s32[]{:S(2)}) async-start(), calls=%async_computation.5 | async-start | bytes 5263360 | tf_op jit(solution)/shard_map/all_gather | solution.py:42
  8.7 908.7 %reduce-scatter.3.cloned.1.call-start = ((), (), s32[]{:S(2)}) async-start(), calls=%async_computation.2 | async-start | bytes 1433600 | tf_op jit(solution)/shard_map/reduce_scatter | solution.py:51
  451.4 426.5 %copy-start.1 = (bf16[108,256]{1,0:T(8,128)(2,1)S(1)}, bf16[108,256]{1,0:T(8,128)(2,1)}, u32[]{:S(2)}) copy-start(bf16[108,256]{1,0:T(8,128)(2,1)} %param.9) | copy-start | bytes 165892
  451.4 426.5 %copy-start.2 = (bf16[108,256]{1,0:T(8,128)(2,1)S(1)}, bf16[108,256]{1,0:T(8,128)(2,1)}, u32[]{:S(2)}) copy-start(bf16[108,256]{1,0:T(8,128)(2,1)} %param.8) | copy-start | bytes 165892
  451.4 508.5 %reduce-scatter.5.cloned.1.call-start = ((), (), s32[]{:S(2)}) async-start(), calls=%async_computation.3 | async-start | bytes 1433600 | tf_op jit(solution)/shard_map/reduce_scatter | solution.py:54
  877.9 4.3 copy-start.5
Sparse Core Ops, SparseCore 0:
  10.8 435.9 all-gather.4
  449.5 423.6 all-gather.6
  876.7 40.6 reduce-scatter.2
  920.7 39.2 reduce-scatter.4
where the time goes:
time: 969 us; the launch traced here: 968 us
  waiting for transfers between devices  933 us (96%)
  matrix products  17.7 us (2%)
  between operations  13.8 us (1%)
    all_gather x1, waiting for transfers between devices, on_device(): lax.all_gather(actor_cotangent, 'fsdp', axis=0, tiled=True)  438 us
    all_gather x1, waiting for transfers between devices, on_device(): lax.all_gather(critic_cotangent, 'fsdp', axis=0, tiled=True)  422 us
    reduce_scatter x1, waiting for transfers between devices, on_device(): lax.psum_scatter(critic_wpart.astype(jnp.bfloat16), 'dp', scatter_dimensi...  40.8 us
    reduce_scatter x1, waiting for transfers between devices, on_device(): lax.psum_scatter(actor_wpart.astype(jnp.bfloat16), 'dp', scatter_dimensio...  31 us
  transfers between devices with their start and end apart: 4, of which 4 were waited for; matrix products, arithmetic and copies ran while one was open for 2% of the time, Pallas kernels for 0%

commit v1 on v0

v1 whole, which is shorter than its diff:
```python
import jax
import jax.numpy as jnp
from jax import lax
from jax.experimental import pallas as pl
from jax.experimental.pallas import tpu as pltpu
from jax.sharding import PartitionSpec as P

MESH = pl.DeviceIdType.MESH
BF16, F32 = jnp.bfloat16, jnp.float32

N_DP, NX, NLO, NZ = 4, 8, 2, 8
FF, TOK, D = 108, 256, 5120
COLS = D // N_DP
HALF = COLS // 2
PAD = 112
ROWS = 2 * PAD


def fsdp_index(x, lo, z, core):
    return ((x * NLO + lo) * NZ + z) * 2 + core


def permutation():
    j = lax.broadcasted_iota(jnp.int32, (TOK, TOK), 0)
    place = lax.broadcasted_iota(jnp.int32, (TOK, TOK), 1)
    moved = ((j >> 3) & 1) * 128 + (j >> 5) * 16 + ((j >> 4) & 1) * 8 + (j & 7)
    return jnp.where(moved == place, 1.0, 0.0).astype(BF16)


def kernel(
    a_gate, a_up, a_cot, a_down, c_gate, c_up, c_cot, c_down,
    a_w, a_g, a_u, c_w, c_g, c_u,
    row_in, row_out, row_got, stage,
    gate2, up2, down2, down, gate_p, up_p, hid, cot_a, cot_b,
    hacc, wacc_a, wacc_b, wout, hsend, hgot, gout, uout,
    load_sem, sib_send, sib_recv, p0_send, p0_recv, p1_send, p1_recv,
    ring_send, ring_recv, hid_send, hid_recv, rs_send, rs_recv, out_sem, out_send, out_recv,
):
    k = lax.axis_index("dp")
    f = lax.axis_index("fsdp")
    core = f % 2
    z = (f // 2) % NZ
    lo = (f // (2 * NZ)) % NLO
    x = f // (2 * NZ * NLO)
    zq, zs = z // 4, z % 4
    sib = (k, f + 1 - 2 * core)

    def by_core(fn):
        @pl.when(core == 0)
        def _():
            fn(0)

        @pl.when(core == 1)
        def _():
            fn(1)

    gates, ups, downs = (a_gate, c_gate), (a_up, c_up), (a_down, c_down)
    cot_rows = (a_cot, c_cot)
    columns = pl.ds(pl.multiple_of(k * COLS, 128), COLS)

    row_loads = [pltpu.make_async_copy(cot_rows[m], row_in.at[m], load_sem.at[m]) for m in range(2)]
    for copy in row_loads:
        copy.start()

    def own_loads(m):
        return (
            pltpu.make_async_copy(gates[m], gate2.at[m], load_sem.at[2]),
            pltpu.make_async_copy(ups[m], up2.at[m], load_sem.at[3]),
            pltpu.make_async_copy(downs[m].at[:, columns], down2.at[m], load_sem.at[4]),
        )

    by_core(lambda m: [copy.start() for copy in own_loads(m)])

    barrier = pltpu.get_barrier_semaphore()

    def greet(dp, fs):
        pl.semaphore_signal(barrier, inc=1, device_id=(dp, fs), device_id_type=MESH)

    own_p0 = zs == k
    for s in range(16):
        s_lo, s_z, s_core = s // 8, (s // 2) % 4, s % 2
        source = fsdp_index(x, s_lo, zq * 4 + s_z, s_core)

        @pl.when(jnp.logical_not((zs == k) & (source == f)))
        def _():
            greet(zs, source)

    for d in range(1, 8):
        greet(k, fsdp_index((x + d) % NX, lo, z, core))
        greet(k, fsdp_index(x, lo, (z + d) % NZ, core))
    for d in range(1, 4):
        greet((k + d) % N_DP, f)
    greet(*sib)

    for m in range(2):
        row_loads[m].wait()
        for b in range(N_DP):
            row_out[2 * b + m] = row_in[m, :, b * COLS:(b + 1) * COLS].astype(F32)

    pl.semaphore_wait(barrier, 34 - jnp.where(own_p0, 1, 0))

    mine = lo * 8 + zs * 2 + core
    stage0 = []
    for t in range(16):
        t_k, t_lo, t_core = t // 4, (t // 2) % 2, t % 2
        target = fsdp_index(x, t_lo, zq * 4 + k, t_core)
        is_self = (k == t_k) & (target == f)
        remote = pltpu.make_async_remote_copy(
            row_out.at[2 * t_k + t_core], row_got.at[mine], p0_send.at[t], p0_recv,
            device_id=(t_k, target), device_id_type=MESH)
        stage0.append((is_self, remote))

        @pl.when(is_self)
        def _(t_k=t_k, t_core=t_core):
            pltpu.make_async_copy(row_out.at[2 * t_k + t_core], row_got.at[mine], p0_recv).start()

        @pl.when(jnp.logical_not(is_self))
        def _(remote=remote):
            remote.start()

    def sibling_pushes(m):
        other = 1 - m
        return [
            pltpu.make_async_remote_copy(src, dst.at[m], sib_send.at[i], sib_recv.at[i], device_id=sib, device_id_type=MESH)
            for i, (src, dst) in enumerate((
                (gates[other], gate2), (ups[other], up2), (downs[other].at[:, columns], down2)))
        ]

    by_core(lambda m: [copy.start() for copy in sibling_pushes(m)])

    perm = permutation()

    pltpu.make_async_copy(row_got, row_got, p0_recv).wait()
    for r in range(16):
        stage[r:r + 1, :] = row_got[r]
    block = stage[...].astype(BF16)
    cot_a[z, x] = block[:, :HALF]
    cot_b[z, x] = block[:, HALF:]

    stage1 = []
    for d in range(1, 8):
        for i, (buf, target) in enumerate((
                (cot_a, fsdp_index((x + d) % NX, lo, z, core)), (cot_b, fsdp_index(x, lo, (z + d) % NZ, core)))):
            copy = pltpu.make_async_remote_copy(
                buf.at[z, x], buf.at[z, x], p1_send.at[i, d - 1], p1_recv.at[i], device_id=(k, target), device_id_type=MESH)
            copy.start()
            stage1.append(copy)

    def own_waits(m):
        for copy in own_loads(m):
            copy.wait()

    by_core(own_waits)
    by_core(lambda m: [copy.wait() for copy in sibling_pushes(m)])
    for h in range(2):
        rows = slice(h * PAD, h * PAD + FF)
        gate32 = jnp.dot(gate2[h], perm, preferred_element_type=F32)
        up32 = jnp.dot(up2[h], perm, preferred_element_type=F32)
        gate_p[rows, :] = gate32
        up_p[rows, :] = up32
        hidden = (gate32 * jax.nn.sigmoid(gate32) * up32).astype(BF16)
        hid[k, 0, rows, :] = hidden[:, :128]
        hid[k, 1, rows, :] = hidden[:, 128:]
        down[rows, :] = down2[h]

    hid_copies = []
    for d in range(1, 4):
        copy = pltpu.make_async_remote_copy(
            hid.at[k], hid.at[k], hid_send.at[d - 1], hid_recv.at[d - 1],
            device_id=((k + d) % N_DP, f), device_id_type=MESH)
        copy.start()
        hid_copies.append(copy)

    for i, buf in enumerate((cot_a, cot_b)):
        whole = buf.at[0, pl.ds(0, 7)]
        pltpu.make_async_copy(whole, whole, p1_recv.at[i]).wait()

    def ring_copy(flow, step):
        forward = flow % 2 == 0
        shift = -step if forward else step
        if flow < 2:
            unit = (z + shift + NZ) % NZ
            ref = cot_a.at[unit] if step < 3 else cot_a.at[unit, pl.ds(0 if forward else 4, 4)]
            target = fsdp_index(x, lo, (z + (1 if forward else NZ - 1)) % NZ, core)
        else:
            unit = (x + shift + NX) % NX
            ref = cot_b.at[:, unit] if step < 3 else cot_b.at[pl.ds(0 if forward else 4, 4), unit]
            target = fsdp_index((x + (1 if forward else NX - 1)) % NX, lo, z, core)
        return pltpu.make_async_remote_copy(
            ref, ref, ring_send.at[flow, step], ring_recv.at[flow, step], device_id=(k, target), device_id_type=MESH)

    rings = []
    for step in range(4):
        for flow in range(4):
            if step:
                rings[4 * (step - 1) + flow].wait_recv()
            copy = ring_copy(flow, step)
            copy.start()
            rings.append(copy)
    for flow in range(4):
        rings[12 + flow].wait_recv()

    def hidden_partial(unit):
        both = []
        for buf, part in ((cot_a, slice(0, HALF)), (cot_b, slice(HALF, COLS))):
            both.append(lax.dot_general(
                down[:, part], buf[unit].reshape(128, HALF), (((1,), (1,)), ((), ())), preferred_element_type=F32))
        return both[0] + both[1]

    rs_copies = []
    for d in range(1, 4):
        group = (k + d) % N_DP
        for q in range(2):
            hsend[d - 1, q] = hidden_partial(q * 4 + group).astype(BF16)
        copy = pltpu.make_async_remote_copy(
            hsend.at[d - 1], hgot.at[d - 1], rs_send.at[d - 1], rs_recv.at[d - 1], device_id=(group, f), device_id_type=MESH)
        copy.start()
        rs_copies.append(copy)
    for q in range(2):
        hacc[q] = hidden_partial(q * 4 + k)

    for copy in hid_copies:
        copy.wait_recv()
    for buf, acc, part in ((cot_a, wacc_a, slice(0, HALF)), (cot_b, wacc_b, slice(HALF, COLS))):
        for unit in range(8):
            term = jnp.dot(hid[unit % 4, unit // 4], buf[unit].reshape(128, HALF), preferred_element_type=F32)
            if unit == 0:
                acc[...] = term
            elif unit < 7:
                acc[...] += term
            else:
                term = acc[...] + term
                wout[0, :, part] = term[:FF]
                wout[1, :, part] = term[PAD:PAD + FF]

    weights, ggrads, ugrads = (a_w, c_w), (a_g, c_g), (a_u, c_u)

    def out_copies(m, i, src, outs):
        return (
            pltpu.make_async_copy(src.at[m], outs[m], out_sem.at[i]),
            pltpu.make_async_remote_copy(
                src.at[1 - m], outs[m], out_send.at[i], out_recv.at[i], device_id=sib, device_id_type=MESH),
        )

    by_core(lambda m: [copy.start() for copy in out_copies(m, 0, wout, weights)])

    for copy in rs_copies:
        copy.wait_recv()
    halves_g, halves_u = [], []
    for q in range(2):
        lanes = slice(q * 128, (q + 1) * 128)
        grad = hacc[q] + hgot[0, q].astype(F32) + hgot[1, q].astype(F32) + hgot[2, q].astype(F32)
        gate32, up32 = gate_p[:, lanes], up_p[:, lanes]
        sig = jax.nn.sigmoid(gate32)
        halves_g.append((grad * up32 * sig * (1.0 + gate32 * (1.0 - sig))).astype(BF16))
        halves_u.append((grad * (gate32 * sig)).astype(BF16))
    perm = permutation()
    for halves, out in ((halves_g, gout), (halves_u, uout)):
        back = lax.dot_general(
            jnp.concatenate(halves, axis=1), perm, (((1,), (1,)), ((), ())), preferred_element_type=F32).astype(BF16)
        out[0] = back[:FF]
        out[1] = back[PAD:PAD + FF]

    by_core(lambda m: [copy.start() for copy in out_copies(m, 1, gout, ggrads)])
    by_core(lambda m: [copy.start() for copy in out_copies(m, 2, uout, ugrads)])

    for is_self, copy in stage0:
        @pl.when(jnp.logical_not(is_self))
        def _(copy=copy):
            copy.wait_send()
    for copy in stage1 + hid_copies + rings + rs_copies:
        copy.wait_send()

    def finish(m):
        for i, (src, outs) in enumerate(((wout, weights), (gout, ggrads), (uout, ugrads))):
            local, remote = out_copies(m, i, src, outs)
            local.wait()
            remote.wait_send()
            pltpu.make_async_remote_copy(
                src.at[m], outs[1 - m], out_send.at[i], out_recv.at[i], device_id=sib, device_id_type=MESH).wait_recv()

    by_core(finish)


def on_device(*args):
    any_spec = pl.BlockSpec(memory_space=pl.ANY)
    dma, vmem = pltpu.SemaphoreType.DMA, pltpu.VMEM
    weight = jax.ShapeDtypeStruct((FF, COLS), F32)
    small = jax.ShapeDtypeStruct((FF, TOK), BF16)
    return pl.pallas_call(
        kernel,
        out_shape=(weight, small, small, weight, small, small),
        in_specs=[any_spec] * 8,
        out_specs=(any_spec,) * 6,
        scratch_shapes=[
            vmem((2, 1, D), BF16),
            vmem((8, 1, COLS), F32),
            vmem((16, 1, COLS), F32),
            vmem((16, COLS), F32),
            vmem((2, FF, TOK), BF16),
            vmem((2, FF, TOK), BF16),
            vmem((2, FF, COLS), BF16),
            vmem((ROWS, COLS), BF16),
            vmem((ROWS, TOK), F32),
            vmem((ROWS, TOK), F32),
            vmem((N_DP, 2, ROWS, 128), BF16),
            vmem((NZ, NX, 16, HALF), BF16),
            vmem((NZ, NX, 16, HALF), BF16),
            vmem((2, ROWS, 128), F32),
            vmem((ROWS, HALF), F32),
            vmem((ROWS, HALF), F32),
            vmem((2, FF, COLS), F32),
            vmem((3, 2, ROWS, 128), BF16),
            vmem((3, 2, ROWS, 128), BF16),
            vmem((2, FF, TOK), BF16),
            vmem((2, FF, TOK), BF16),
            dma((5,)),
            dma((3,)),
            dma((3,)),
            dma((16,)),
            dma,
            dma((2, 7)),
            dma((2,)),
            dma((4, 4)),
            dma((4, 4)),
            dma((3,)),
            dma((3,)),
            dma((3,)),
            dma((3,)),
            dma((3,)),
            dma((3,)),
            dma((3,)),
        ],
        compiler_params=pltpu.CompilerParams(
            collective_id=0, has_side_effects=True, vmem_limit_bytes=40 * 1024 * 1024),
        cost_estimate=pl.CostEstimate(flops=1_200_000_000, bytes_accessed=4_000_000, transcendentals=200_000),
        name="mlp_backward",
    )(*args)


def solution(mesh):
    placed = (
        P("fsdp", "dp"),
        P("fsdp", "dp"),
        P(("dp", "fsdp"), None),
        P("fsdp", None),
    )
    return jax.shard_map(
        on_device,
        mesh=mesh,
        in_specs=placed * 2,
        out_specs=(P("fsdp", "dp"),) * 6,
        check_vma=False,
    )
```

time: 969 us -> 83.1 us (0.09)
  waiting for transfers between devices: 933 us -> 0 us
  Pallas kernels: 0 us -> 70.6 us
  matrix products: 17.7 us -> 0 us
  between operations: 13.8 us -> 0.66 us
  local copies, waits for them, and re-layouts: 0.04 us -> 11.3 us
    all_gather x2 -> x0, waiting for transfers between devices: 860 us -> none  [the longest x1 438 us: on_device(): lax.all_gather(actor_cotangent, 'fsdp', axis=0, tiled=True)]
    reduce_scatter x2 -> x0, waiting for transfers between devices: 71.8 us -> none  [the longest x1 40.8 us: on_device(): lax.psum_scatter(critic_wpart.astype(jnp.bfloat16), 'dp', scatter_dimensi...]
    pallas_call x0 -> x1, Pallas kernels: none -> 70.6 us  [on_device(): pl.pallas_call(kernel, out_shape=(weight, small, small, weight, small, sm...]
    dot_general x4 -> x0, matrix products: 17.7 us -> none  [the longest x2 8.48 us: back_project(): lax.dot_general(down, rows, (((1,), (1,)), ((), ())), preferred_element_t...]
    unnamed x12 -> x22, local copies, waits for them, and re-layouts: 0.04 us -> 11.3 us
  transfers between devices with their start and end apart: 4 -> 0, of which waited for: 4 -> 0; matrix products, arithmetic and copies ran while one was open for 2% -> 0% of each run, Pallas kernels for 0% -> 0%
where the time goes in v1:
time: 83.1 us; the launch traced here: 82.6 us
  Pallas kernels  70.6 us (85%)
  local copies, waits for them, and re-layouts  11.3 us (14%)
    pallas_call x1, Pallas kernels, on_device(): pl.pallas_call(kernel, out_shape=(weight, small, small, weight, small, sm...  70.6 us
    unnamed x22, local copies, waits for them, and re-layouts  11.3 us

profile of v1, /device:TPU:1, one launch (start us, length us, event | category | flops | bytes accessed | tf_op | source)
XLA Modules:
  0.0 82.6 jit_solution(17081526003575389583)
XLA Ops:
  0.6 0.0 copy-start
  0.6 1.2 %copy-done = bf16[108,5120]{1,0:T(8,128)(2,1)S(1)} copy-done((bf16[108,5120]{1,0:T(8,128)(2,1)S(1)}, bf16[108,5120]{1,0:T(8,128)(2,1)}, u32[]{:S(2)}) %copy-start) | copy-done | bytes 1105944
  1.9 0.0 copy-start.1
  1.9 1.3 %copy-done.1 = bf16[108,5120]{1,0:T(8,128)(2,1)S(1)} copy-done((bf16[108,5120]{1,0:T(8,128)(2,1)S(1)}, bf16[108,5120]{1,0:T(8,128)(2,1)}, u32[]{:S(2)}) %copy-start.1) | copy-done | bytes 1105944
  3.2 0.0 copy-start.2
  3.2 0.8 copy-done.2
  4.0 0.0 copy-start.3
  4.0 0.8 copy-done.3
  4.8 0.0 copy-start.4
  4.8 0.8 copy-done.4
  5.6 0.0 copy-start.5
  5.6 0.8 copy-done.5
  6.4 0.0 copy-start.6
  6.4 0.7 copy-done.6
  7.2 0.0 copy-start.7
  7.2 0.7 copy-done.7
  7.9 70.6 %mlp_backward.1 = (f32[108,1280]{1,0:T(8,128)S(1)}, bf16[108,256]{1,0:T(8,128)(2,1)S(1)}, bf16[108,256]{1,0:T(8,128)(2,1)S(1)}, f32[108,1280]{1,0:T(8,128)S(1)},...) custom-call(bf16[108,256]{1,0:T(8,128)(2,1)S(1)} %copy-done.2, bf16[108,256]{1,0:T(8,128)(2,1)S(1)} %copy-done.3, ...), custom_call_target="tpu_custom_call" | custom-call | flops 1200000000 | bytes 4000000 | tf_op jit(solution)/shard_map/mlp_backward/pallas_call | solution.py:290
  78.5 0.8 copy.20
  79.3 0.6 copy.21
  79.9 0.6 copy.22
  80.5 0.8 copy.23
  81.3 0.6 copy.24
  82.0 0.6 copy.25
Async XLA Ops:
  0.6 1.3 %copy-start = (bf16[108,5120]{1,0:T(8,128)(2,1)S(1)}, bf16[108,5120]{1,0:T(8,128)(2,1)}, u32[]{:S(2)}) copy-start(bf16[108,5120]{1,0:T(8,128)(2,1)} %a_down.1) | copy-start | bytes 3317764
  1.9 1.3 %copy-start.1 = (bf16[108,5120]{1,0:T(8,128)(2,1)S(1)}, bf16[108,5120]{1,0:T(8,128)(2,1)}, u32[]{:S(2)}) copy-start(bf16[108,5120]{1,0:T(8,128)(2,1)} %c_down.1) | copy-start | bytes 3317764
  3.2 0.8 copy-start.2
  4.0 0.8 copy-start.3
  4.8 0.8 copy-start.4
  5.6 0.8 copy-start.5
  6.4 0.7 copy-start.6
  7.2 0.7 copy-start.7

commit v2 on v1

v2 whole, which is shorter than its diff:
```python
import jax
import jax.numpy as jnp
from jax import lax
from jax.experimental import pallas as pl
from jax.experimental.pallas import tpu as pltpu
from jax.sharding import PartitionSpec as P

MESH = pl.DeviceIdType.MESH
BF16, F32 = jnp.bfloat16, jnp.float32

N_DP, NX, NLO, NZ = 4, 8, 2, 8
FF, TOK, D = 108, 256, 5120
COLS = D // N_DP
PAD = 112
ROWS = 2 * PAD
LANES = 256
CHUNKS = 2
PART = 4 // CHUNKS
VMEM_LIMIT = 58 * 1024 * 1024


def fsdp_index(x, lo, z, core):
    return ((x * NLO + lo) * NZ + z) * 2 + core


def permutation(k):
    j = lax.broadcasted_iota(jnp.int32, (TOK, TOK), 0)
    place = lax.broadcasted_iota(jnp.int32, (TOK, TOK), 1)
    kind = ((j >> 5) + k) & 1
    moved = ((j >> 3) & 1) * 128 + kind * 64 + (j >> 6) * 16 + ((j >> 4) & 1) * 8 + (j & 7)
    return jnp.where(moved == place, 1.0, 0.0).astype(BF16)


def kernel(
    a_gate, a_up, a_cot, a_down, c_gate, c_up, c_cot, c_down,
    a_w, a_g, a_u, c_w, c_g, c_u,
    row_in, row_out, row_got, stage,
    gate2, up2, down2, down, gate_f, up_f, hid, cot,
    hown, hsend_a, hsend_b, hgot, wout, gout, uout,
    load_sem, sib_send, sib_recv, p0_send, p0_recv, p1_send, p1_recv,
    ring_send, ring_recv, hid_send, hid_recv, rs_send, rs_recv, out_sem, out_send, out_recv,
):
    k = lax.axis_index("dp")
    f = lax.axis_index("fsdp")
    core = f % 2
    z = (f // 2) % NZ
    lo = (f // (2 * NZ)) % NLO
    x = f // (2 * NZ * NLO)
    zq, zs = z // 4, z % 4
    kind, xh = (x + z) % 2, x // 2
    sib = (k, f + 1 - 2 * core)

    def by_core(fn):
        @pl.when(core == 0)
        def _():
            fn(0)

        @pl.when(core == 1)
        def _():
            fn(1)

    gates, ups, downs = (a_gate, c_gate), (a_up, c_up), (a_down, c_down)
    cot_rows = (a_cot, c_cot)
    columns = pl.ds(pl.multiple_of(k * COLS, 128), COLS)

    row_loads = [pltpu.make_async_copy(cot_rows[m], row_in.at[m], load_sem.at[m]) for m in range(2)]
    for copy in row_loads:
        copy.start()

    def own_loads(m):
        return (
            pltpu.make_async_copy(gates[m], gate2.at[m], load_sem.at[2]),
            pltpu.make_async_copy(ups[m], up2.at[m], load_sem.at[3]),
            pltpu.make_async_copy(downs[m].at[:, columns], down2.at[m], load_sem.at[4]),
        )

    by_core(lambda m: [copy.start() for copy in own_loads(m)])

    barrier = pltpu.get_barrier_semaphore()

    def greet(dp, fs):
        pl.semaphore_signal(barrier, inc=1, device_id=(dp, fs), device_id_type=MESH)

    own_p0 = zs == k
    for s in range(16):
        s_lo, s_z, s_core = s // 8, (s // 2) % 4, s % 2
        source = fsdp_index(x, s_lo, zq * 4 + s_z, s_core)

        @pl.when(jnp.logical_not((zs == k) & (source == f)))
        def _():
            greet(zs, source)

    for i in range(4):
        @pl.when((kind == 1) | (i > 0))
        def _(i=i):
            greet(k, fsdp_index((x + 2 * i + kind) % NX, lo, z, core))

        @pl.when((kind == 0) | (i > 0))
        def _(i=i):
            greet(k, fsdp_index(x, lo, (z + 2 * i + 1 - kind) % NZ, core))

    for step in (1, NX - 1):
        greet(k, fsdp_index((x + step) % NX, lo, z, core))
        greet(k, fsdp_index(x, lo, (z + step) % NZ, core))
    for d in range(1, 4):
        greet((k + d) % N_DP, f)
    greet(*sib)

    for m in range(2):
        row_loads[m].wait()
        for b in range(N_DP):
            row_out[2 * b + m] = row_in[m, :, b * COLS:(b + 1) * COLS].astype(F32)

    pl.semaphore_wait(barrier, 31 - jnp.where(own_p0, 1, 0))

    mine = lo * 8 + zs * 2 + core
    stage0 = []
    for t in range(16):
        t_k, t_lo, t_core = t // 4, (t // 2) % 2, t % 2
        target = fsdp_index(x, t_lo, zq * 4 + k, t_core)
        is_self = (k == t_k) & (target == f)
        remote = pltpu.make_async_remote_copy(
            row_out.at[2 * t_k + t_core], row_got.at[mine], p0_send.at[t], p0_recv,
            device_id=(t_k, target), device_id_type=MESH)
        stage0.append((is_self, remote))

        @pl.when(is_self)
        def _(t_k=t_k, t_core=t_core):
            pltpu.make_async_copy(row_out.at[2 * t_k + t_core], row_got.at[mine], p0_recv).start()

        @pl.when(jnp.logical_not(is_self))
        def _(remote=remote):
            remote.start()

    def sibling_pushes(m):
        other = 1 - m
        return [
            pltpu.make_async_remote_copy(src, dst.at[m], sib_send.at[i], sib_recv.at[i], device_id=sib, device_id_type=MESH)
            for i, (src, dst) in enumerate((
                (gates[other], gate2), (ups[other], up2), (downs[other].at[:, columns], down2)))
        ]

    by_core(lambda m: [copy.start() for copy in sibling_pushes(m)])

    perm = permutation(k)

    pltpu.make_async_copy(row_got, row_got, p0_recv).wait()
    for r in range(16):
        stage[r:r + 1, :] = row_got[r]
    cot[zq, zs // 2, zs % 2, kind, xh] = stage[...].astype(BF16)

    own_block = cot.at[zq, zs // 2, zs % 2, kind, xh]
    stage1 = []
    for d in (4, 5, 3, 6, 2, 7, 1):
        target = jnp.where(
            kind == 0, fsdp_index((x + d) % NX, lo, z, core), fsdp_index(x, lo, (z + d) % NZ, core))
        copy = pltpu.make_async_remote_copy(
            own_block, own_block, p1_send.at[d - 1], p1_recv.at[kind], device_id=(k, target), device_id_type=MESH)
        copy.start()
        stage1.append(copy)

    def own_waits(m):
        for copy in own_loads(m):
            copy.wait()

    by_core(own_waits)
    by_core(lambda m: [copy.wait() for copy in sibling_pushes(m)])
    for h in range(2):
        rows = slice(h * PAD, h * PAD + FF)
        gate32 = jnp.dot(gate2[h], perm, preferred_element_type=F32)
        up32 = jnp.dot(up2[h], perm, preferred_element_type=F32)
        hidden = (gate32 * jax.nn.sigmoid(gate32) * up32).astype(BF16)
        hid[k, 0, rows, :] = hidden[:, :128]
        hid[k, 1, rows, :] = hidden[:, 128:]
        down[h * 128:h * 128 + FF, :] = down2[h]

    hid_copies = []
    for d in range(1, 4):
        copy = pltpu.make_async_remote_copy(
            hid.at[k], hid.at[k], hid_send.at[d - 1], hid_recv.at[d - 1],
            device_id=((k + d) % N_DP, f), device_id_type=MESH)
        copy.start()
        hid_copies.append(copy)

    for i in range(2):
        three, four = cot.at[0, 0, 0, 0, pl.ds(0, 3)], cot.at[0, 0, 0, 0]

        @pl.when(kind == i)
        def _(i=i, three=three):
            pltpu.make_async_copy(three, three, p1_recv.at[i]).wait()

        @pl.when(kind != i)
        def _(i=i, four=four):
            pltpu.make_async_copy(four, four, p1_recv.at[i]).wait()

    def ring_copy(flow, chunk, step):
        forward = flow % 2 == 0
        shift = -step if forward else step
        part = pl.ds(chunk * PART, PART)
        if flow < 2:
            unit = (z + shift + NZ) % NZ
            ref = cot.at[unit // 4, (unit // 2) % 2, unit % 2, 0, part]
            target = fsdp_index(x, lo, (z + (1 if forward else NZ - 1)) % NZ, core)
        else:
            unit = (x + shift + NX) % NX
            ref = cot.at[chunk, :, 1 - unit % 2, 1, unit // 2]
            target = fsdp_index((x + (1 if forward else NX - 1)) % NX, lo, z, core)
        return pltpu.make_async_remote_copy(
            ref, ref, ring_send.at[flow, chunk, step], ring_recv.at[flow, chunk, step],
            device_id=(k, target), device_id_type=MESH)

    def hidden_partial(block):
        return lax.dot_general(
            block.reshape(64, COLS), down[...], (((1,), (1,)), ((), ())), preferred_element_type=F32)

    def to_group(group, src, piece):
        apart = (group + N_DP - k) % N_DP

        @pl.when(apart != 0)
        def _():
            pltpu.make_async_remote_copy(
                src, piece(hgot.at[apart - 1]), rs_send, rs_recv, device_id=(group, f), device_id_type=MESH).start()

        return apart == 0

    def unit_a(unit):
        unit = (unit + NZ) % NZ
        group, q = unit % 4, unit // 4
        grad = hidden_partial(cot[q, group // 2, group % 2, 0]).reshape(4, 16, LANES)
        hsend_a[unit] = grad.astype(BF16)

        @pl.when(to_group(group, hsend_a.at[unit], lambda ref: ref.at[q, 0]))
        def _():
            hown[q, 0] = grad

    def unit_b(unit):
        unit = (unit + NX) % NX
        low = 1 - unit % 2
        grad = hidden_partial(cot[:, :, low, 1, unit // 2]).reshape(2, 2, 16, LANES)
        hsend_b[unit] = grad.astype(BF16)
        for high in range(2):
            @pl.when(to_group(2 * high + low, hsend_b.at[unit, :, high], lambda ref: ref.at[:, 1, unit // 2]))
            def _(high=high):
                hown[:, 1, unit // 2] = grad[:, high]

    rings = {}
    for step in range(5):
        for chunk in range(CHUNKS):
            for flow in range(4):
                if (flow, chunk, step - 1) in rings:
                    rings[flow, chunk, step - 1].wait_recv()
                if step < 3 or step == 3 and (chunk < CHUNKS // 2) == (flow % 2 == 0):
                    rings[flow, chunk, step] = ring_copy(flow, chunk, step)
                    rings[flow, chunk, step].start()
        if step == 0:
            for h in range(2):
                gate32 = lax.dot_general(perm, gate2[h], (((0,), (1,)), ((), ())), preferred_element_type=F32)
                up32 = lax.dot_general(perm, up2[h], (((0,), (1,)), ((), ())), preferred_element_type=F32)
                sig = jax.nn.sigmoid(gate32)
                gate_f[:, h * 128:h * 128 + FF] = up32 * sig * (1.0 + gate32 * (1.0 - sig))
                up_f[:, h * 128:h * 128 + FF] = gate32 * sig
        for shift in (-step, step) if 0 < step < 4 else (step,):
            unit_a(z + shift)
            unit_b(x + shift)

    for copy in hid_copies:
        copy.wait_recv()
    for n in range(COLS // 256):
        part = slice(n * 256, (n + 1) * 256)
        total = None
        for group in range(N_DP):
            left = jnp.concatenate([hid[group, 0], hid[group, 1]], axis=1)
            right = jnp.concatenate(
                [cot[q, group // 2, group % 2, :, :, :, part].reshape(128, 256) for q in range(2)], axis=0)
            term = jnp.dot(left, right, preferred_element_type=F32)
            total = term if total is None else total + term
        wout[0, :, part] = total[:FF]
        wout[1, :, part] = total[PAD:PAD + FF]

    weights, ggrads, ugrads = (a_w, c_w), (a_g, c_g), (a_u, c_u)

    def out_copies(m, i, src, outs):
        return (
            pltpu.make_async_copy(src.at[m], outs[m], out_sem.at[i]),
            pltpu.make_async_remote_copy(
                src.at[1 - m], outs[m], out_send.at[i], out_recv.at[i], device_id=sib, device_id_type=MESH),
        )

    by_core(lambda m: [copy.start() for copy in out_copies(m, 0, wout, weights)])

    pltpu.make_async_copy(hgot, hgot, rs_recv).wait()
    grad = hown[...]
    for i in range(3):
        grad = grad + hgot[i].astype(F32)
    grad = grad.reshape(TOK, LANES)
    perm = permutation(k)
    for factor, out in ((gate_f, gout), (up_f, uout)):
        back = lax.dot_general(
            (grad * factor[...]).astype(BF16), perm, (((0,), (1,)), ((), ())), preferred_element_type=F32).astype(BF16)
        out[0] = back[:FF]
        out[1] = back[128:128 + FF]

    by_core(lambda m: [copy.start() for copy in out_copies(m, 1, gout, ggrads)])
    by_core(lambda m: [copy.start() for copy in out_copies(m, 2, uout, ugrads)])

    for is_self, copy in stage0:
        @pl.when(jnp.logical_not(is_self))
        def _(copy=copy):
            copy.wait_send()
    for copy in stage1 + hid_copies + list(rings.values()):
        copy.wait_send()
    pltpu.make_async_copy(hgot, hgot, rs_send).wait()

    def finish(m):
        for i, (src, outs) in enumerate(((wout, weights), (gout, ggrads), (uout, ugrads))):
            local, remote = out_copies(m, i, src, outs)
            local.wait()
            remote.wait_send()
            pltpu.make_async_remote_copy(
                src.at[m], outs[1 - m], out_send.at[i], out_recv.at[i], device_id=sib, device_id_type=MESH).wait_recv()

    by_core(finish)


def store(*refs):
    ins, outs, held, (in_sem, out_sem) = refs[:6], refs[6:12], refs[12:18], refs[18:]
    loads = [pltpu.make_async_copy(ins[i], held[i], in_sem.at[i]) for i in range(6)]
    stores = [pltpu.make_async_copy(held[i], outs[i], out_sem.at[i]) for i in range(6)]
    for copy in loads:
        copy.start()
    for load, copy in zip(loads, stores):
        load.wait()
        copy.start()
    for copy in stores:
        copy.wait()


def on_device(*args):
    hbm_spec = pl.BlockSpec(memory_space=pltpu.HBM)
    dma, vmem = pltpu.SemaphoreType.DMA, pltpu.VMEM
    weight = jax.ShapeDtypeStruct((FF, COLS), F32)
    small = jax.ShapeDtypeStruct((FF, TOK), BF16)
    results = pl.pallas_call(
        kernel,
        out_shape=(weight, small, small, weight, small, small),
        in_specs=[hbm_spec] * 8,
        out_specs=(hbm_spec,) * 6,
        scratch_shapes=[
            vmem((2, 1, D), BF16),
            vmem((8, 1, COLS), F32),
            vmem((16, 1, COLS), F32),
            vmem((16, COLS), F32),
            vmem((2, FF, TOK), BF16),
            vmem((2, FF, TOK), BF16),
            vmem((2, FF, COLS), BF16),
            vmem((LANES, COLS), BF16),
            vmem((TOK, LANES), F32),
            vmem((TOK, LANES), F32),
            vmem((N_DP, 2, ROWS, 128), BF16),
            vmem((2, 2, 2, 2, 4, 16, COLS), BF16),
            vmem((2, 2, 4, 16, LANES), F32),
            vmem((NZ, 4, 16, LANES), BF16),
            vmem((NX, 2, 2, 16, LANES), BF16),
            vmem((3, 2, 2, 4, 16, LANES), BF16),
            vmem((2, FF, COLS), F32),
            vmem((2, FF, TOK), BF16),
            vmem((2, FF, TOK), BF16),
            dma((5,)),
            dma((3,)),
            dma((3,)),
            dma((16,)),
            dma,
            dma((7,)),
            dma((2,)),
            dma((4, CHUNKS, 4)),
            dma((4, CHUNKS, 4)),
            dma((3,)),
            dma((3,)),
            dma,
            dma,
            dma((3,)),
            dma((3,)),
            dma((3,)),
        ],
        compiler_params=pltpu.CompilerParams(
            collective_id=0, has_side_effects=True, vmem_limit_bytes=VMEM_LIMIT),
        cost_estimate=pl.CostEstimate(flops=1_200_000_000, bytes_accessed=4_000_000, transcendentals=200_000),
        name="mlp_backward",
    )(*args)
    return pl.pallas_call(
        store,
        out_shape=(weight, small, small, weight, small, small),
        in_specs=[hbm_spec] * 6,
        out_specs=(hbm_spec,) * 6,
        scratch_shapes=[vmem(a.shape, a.dtype) for a in results] + [dma((6,)), dma((6,))],
        compiler_params=pltpu.CompilerParams(vmem_limit_bytes=VMEM_LIMIT),
        name="store_results",
    )(*results)


def solution(mesh):
    placed = (
        P("fsdp", "dp"),
        P("fsdp", "dp"),
        P(("dp", "fsdp"), None),
        P("fsdp", None),
    )
    return jax.shard_map(
        on_device,
        mesh=mesh,
        in_specs=placed * 2,
        out_specs=(P("fsdp", "dp"),) * 6,
        check_vma=False,
    )
```

time: 83.1 us -> 66.5 us (0.80)
  local copies, waits for them, and re-layouts: 11.3 us -> 0 us
  Pallas kernels: 70.6 us -> 65.7 us
    unnamed x22 -> x0, local copies, waits for them, and re-layouts: 11.3 us -> none
    pallas_call x1, Pallas kernels: 70.6 us -> 63.5 us  [on_device(): pl.pallas_call(kernel, out_shape=(weight, small, small, weight, small, sm...]
    pallas_call x0 -> x1, Pallas kernels: none -> 2.22 us  [on_device(): pl.pallas_call(store, out_shape=(weight, small, small, weight, small, sma...]
where the time goes in v2:
time: 66.5 us; the launch traced here: 66.3 us
  Pallas kernels  65.7 us (99%)
    pallas_call x1, Pallas kernels, on_device(): pl.pallas_call(kernel, out_shape=(weight, small, small, weight, small, sm...  63.5 us
    pallas_call x1, Pallas kernels, on_device(): pl.pallas_call(store, out_shape=(weight, small, small, weight, small, sma...  2.22 us

profile of v2, /device:TPU:1, one launch (start us, length us, event | category | flops | bytes accessed | tf_op | source)
XLA Modules:
  0.0 66.3 jit_solution(2669973901003556802)
XLA Ops:
  0.6 63.5 %mlp_backward.1 = (f32[108,1280]{1,0:T(8,128)}, bf16[108,256]{1,0:T(8,128)(2,1)}, bf16[108,256]{1,0:T(8,128)(2,1)}, f32[108,1280]{1,0:T(8,128)}, bf16[108,256]{1,0:T(8,128)(2,1)}, /*index=5*/bf16[108,256]{1,0:T(8,128)(2,1)}) custom-call(bf16[108,256]{1,0:T(8,128)(2,1)} %a_gate.1, bf16[108,256]{1,0:T(8,128)(2,1)} %a_up.1, bf16[1,5120]{1,0:T(2,128)(2,1)} %a_cot.1, ...), custom_call_target="tpu_custom_call" | custom-call | flops 1200000000 | bytes 4000000 | tf_op jit(solution)/shard_map/mlp_backward/pallas_call | solution.py:343
  64.1 2.2 %store_results.1 = (f32[108,1280]{1,0:T(8,128)}, bf16[108,256]{1,0:T(8,128)(2,1)}, bf16[108,256]{1,0:T(8,128)(2,1)}, f32[108,1280]{1,0:T(8,128)}, bf16[108,256]{1,0:T(8,128)(2,1)}, /*index=5*/bf16[108,256]{1,0:T(8,128)(2,1)}) custom-call(f32[108,1280]{1,0:T(8,128)} %get-tuple-element.12.refs_0_, bf16[108,256]{1,0:T(8,128)(2,1)} %get-tuple-element.13.refs_1_, ...), custom_call_target="tpu_custom_call" | custom-call | tf_op jit(solution)/shard_map/store_results/pallas_call | solution.py:390

commit v3 on v2

v3 whole, which is shorter than its diff:
```python
import jax
import jax.numpy as jnp
from jax import lax
from jax.experimental import pallas as pl
from jax.experimental.pallas import tpu as pltpu
from jax.sharding import PartitionSpec as P

MESH = pl.DeviceIdType.MESH
BF16, F32 = jnp.bfloat16, jnp.float32

N_DP, NX, NLO, NZ = 4, 8, 2, 8
FF, TOK, D = 108, 256, 5120
COLS = D // N_DP
PAD = 112
ROWS = 2 * PAD
UNIT = 64
NEAREST = ((0, 2, 6, 4), (1, 7, 3, 5))
VMEM_LIMIT = 58 * 1024 * 1024


def fsdp_index(x, lo, z, core):
    return ((x * NLO + lo) * NZ + z) * 2 + core


def of_type_0(group):
    return (group == 0) | (group == 3)


def permutation(group):
    j = lax.broadcasted_iota(jnp.int32, (TOK, TOK), 0)
    place = lax.broadcasted_iota(jnp.int32, (TOK, TOK), 1)
    x_weight = jnp.where(of_type_0(group), 16, 64)
    moved = (j >> 6) * x_weight + ((j >> 2) & 3) * (80 - x_weight)
    moved = moved + ((j >> 5) & 1) * 8 + ((j >> 4) & 1) * 4 + (j & 3)
    return jnp.where(moved == place, 1.0, 0.0).astype(BF16)


def kernel(
    a_gate, a_up, a_cot, a_down, c_gate, c_up, c_cot, c_down,
    a_w, a_g, a_u, c_w, c_g, c_u,
    row_in, row_out, row_got, stage,
    gate_own, up_own, gate_sib, up_sib, down2, down, gate_f, up_f, hid, cot,
    hown, hsend, hgot, wout, gout, uout,
    load_sem, sib_send, sib_recv, p0_send, p0_recv, p1_send, p1_recv,
    ring_send, ring_recv, hid_send, hid_recv, rs_send, rs_recv, out_sem, out_send, out_recv,
):
    k = lax.axis_index("dp")
    f = lax.axis_index("fsdp")
    core = f % 2
    z = (f // 2) % NZ
    lo = (f // (2 * NZ)) % NLO
    x = f // (2 * NZ * NLO)
    xp, zp = x // 2, z // 2
    kind = (x + z) % 2
    held = x % 2 * 2 + z % 2
    sib = (k, f + 1 - 2 * core)

    def by_core(fn):
        @pl.when(core == 0)
        def _():
            fn(0)

        @pl.when(core == 1)
        def _():
            fn(1)

    gates, ups, downs = (a_gate, c_gate), (a_up, c_up), (a_down, c_down)
    cot_rows = (a_cot, c_cot)
    columns = pl.ds(pl.multiple_of(k * COLS, 128), COLS)

    row_loads = [pltpu.make_async_copy(cot_rows[m], row_in.at[m], load_sem.at[m]) for m in range(2)]
    for copy in row_loads:
        copy.start()

    def model_load(m, i):
        return pltpu.make_async_copy((gates[m], ups[m])[i], (gate_own, up_own)[i].at[m], load_sem.at[2 + 2 * i + m])

    def down_load(m):
        return pltpu.make_async_copy(downs[m].at[:, columns], down2.at[m], load_sem.at[6])

    for m in range(2):
        for i in range(2):
            model_load(m, i).start()
    by_core(lambda m: down_load(m).start())

    barrier = pltpu.get_barrier_semaphore()

    def greet(dp, fs):
        pl.semaphore_signal(barrier, inc=1, device_id=(dp, fs), device_id_type=MESH)

    own_p0 = held == k
    for a in range(16):
        source = fsdp_index(
            x // 2 * 2 + (x + a // 8 + 1) % 2, (lo + a // 4 + 1) % 2, z // 2 * 2 + (z + a // 2 + 1) % 2, (core + a + 1) % 2)
        if a < 15:
            greet(held, source)
        else:
            pl.when(jnp.logical_not(own_p0))(lambda source=source: greet(held, source))

    for i in range(4):
        @pl.when((kind == 1) | (i > 0))
        def _(i=i):
            greet(k, fsdp_index((x + 2 * i + kind) % NX, lo, z, core))

        @pl.when((kind == 0) | (i > 0))
        def _(i=i):
            greet(k, fsdp_index(x, lo, (z + 2 * i + 1 - kind) % NZ, core))

    for step in (1, NX - 1):
        greet(k, fsdp_index((x + step) % NX, lo, z, core))
        greet(k, fsdp_index(x, lo, (z + step) % NZ, core))
    for d in range(1, 4):
        greet((k + d) % N_DP, f)
        greet((k + d) % N_DP, sib[1])
    greet(*sib)

    for m in range(2):
        row_loads[m].wait()
        for b in range(N_DP):
            row_out[2 * b + m] = row_in[m, :, b * COLS:(b + 1) * COLS].astype(F32)

    pl.semaphore_wait(barrier, 34 - jnp.where(own_p0, 1, 0))

    mine = x % 2 * 8 + lo * 4 + z % 2 * 2 + core
    stage0 = []
    for away in (2, 1, 3, 0):
        for a in range(4):
            t_k, t_lo, t_core = (k + away) % N_DP, (lo + a // 2 + 1) % 2, (core + a + 1) % 2
            src = row_out.at[2 * t_k + t_core]
            stage0.append(pltpu.make_async_remote_copy(
                src, row_got.at[mine], p0_send.at[len(stage0)], p0_recv,
                device_id=(t_k, fsdp_index(2 * xp + k // 2, t_lo, 2 * zp + k % 2, t_core)), device_id_type=MESH))
            if len(stage0) < 16:
                stage0[-1].start()
            else:
                pl.when(own_p0)(lambda src=src: pltpu.make_async_copy(src, row_got.at[mine], p0_recv).start())
                pl.when(jnp.logical_not(own_p0))(stage0[-1].start)

    def sibling_push(m, i):
        src = (gates[1 - m], ups[1 - m], downs[1 - m].at[:, columns])[i]
        return pltpu.make_async_remote_copy(
            src, (gate_sib, up_sib, down2.at[m])[i], sib_send.at[i], sib_recv.at[i], device_id=sib, device_id_type=MESH)

    by_core(lambda m: [sibling_push(m, i).start() for i in range(3)])

    perm = permutation(k)

    for m in range(2):
        for i in range(2):
            model_load(m, i).wait()
    for m in range(2):
        gate32 = lax.dot_general(perm, gate_own[m], (((0,), (1,)), ((), ())), preferred_element_type=F32)
        up32 = lax.dot_general(perm, up_own[m], (((0,), (1,)), ((), ())), preferred_element_type=F32)
        sig = jax.nn.sigmoid(gate32)
        gate_f[m, :, :FF] = up32 * sig * (1.0 + gate32 * (1.0 - sig))
        up_f[m, :, :FF] = gate32 * sig

    pltpu.make_async_copy(row_got, row_got, p0_recv).wait()
    for r in range(16):
        stage[r:r + 1, :] = row_got[r]
    unit_at, block_at = jnp.where(kind == 0, zp, xp), jnp.where(kind == 0, xp, zp)
    cot[held, unit_at, block_at] = stage[...].astype(BF16)

    own_block = cot.at[held, unit_at, block_at]
    stage1 = []
    for d in (4, 5, 3, 6, 2, 7, 1):
        target = jnp.where(
            kind == 0, fsdp_index((x + d) % NX, lo, z, core), fsdp_index(x, lo, (z + d) % NZ, core))
        copy = pltpu.make_async_remote_copy(
            own_block, own_block, p1_send.at[d - 1], p1_recv.at[kind, block_at], device_id=(k, target), device_id_type=MESH)
        copy.start()
        stage1.append(copy)

    by_core(lambda m: [sibling_push(m, i).wait() for i in range(2)])
    for h, (gate, up) in enumerate(((gate_own[core], up_own[core]), (gate_sib[...], up_sib[...]))):
        gate32 = jnp.dot(gate, perm, preferred_element_type=F32)
        up32 = jnp.dot(up, perm, preferred_element_type=F32)
        hid[k, h * PAD:h * PAD + FF, :] = (gate32 * jax.nn.sigmoid(gate32) * up32).astype(BF16)

    hid_copies = []
    for d in range(1, 4):
        copy = pltpu.make_async_remote_copy(
            hid.at[k], hid.at[k], hid_send.at[d - 1], hid_recv.at[d - 1],
            device_id=((k + d) % N_DP, f), device_id_type=MESH)
        copy.start()
        hid_copies.append(copy)

    by_core(lambda m: [down_load(m).wait(), sibling_push(m, 2).wait()])
    for h in range(2):
        down[h * 128:h * 128 + FF, :] = down2[h]

    def unit_of(way, index):
        return (3 * (index % 2), index // 2) if way == 0 else (1 + index % 2, index // 2)

    def block_of(flow, i, step):
        shift = -step if flow % 2 == 0 else step
        along, across = (z, x) if flow < 2 else (x, z)
        index = (along + shift + 8) % 8
        has_own = (along + across + step) % 2 == flow // 2
        block = (across + jnp.where(has_own, NEAREST[0][i], NEAREST[1][i])) % 8 // 2
        group, unit = unit_of(flow // 2, index)
        return cot.at[group, unit, block], block

    def ring_copy(flow, i, step):
        forward = flow % 2 == 0
        ref, _ = block_of(flow, i, step)
        if flow < 2:
            target = fsdp_index(x, lo, (z + (1 if forward else NZ - 1)) % NZ, core)
        else:
            target = fsdp_index((x + (1 if forward else NX - 1)) % NX, lo, z, core)
        return pltpu.make_async_remote_copy(
            ref, ref, ring_send.at[flow, i, step], ring_recv.at[flow, i, step],
            device_id=(k, target), device_id_type=MESH)

    def block_wait(way, i):
        ref, at = block_of(2 * way, i, 0)

        def wait():
            pltpu.make_async_copy(ref, ref, p1_recv.at[way, at]).wait()

        if i:
            wait()
        else:
            pl.when(kind != way)(wait)

    def send_partial(way, index):
        index = (index + 8) % 8
        group, unit = unit_of(way, index)
        grad = lax.dot_general(
            cot[group, unit].reshape(UNIT, COLS), down[...], (((1,), (1,)), ((), ())), preferred_element_type=F32)
        apart = (group + N_DP - k) % N_DP
        for h in range(2):
            half = grad[:, h * 128:(h + 1) * 128].reshape(4, 16, 128)
            hsend[way, index, h] = half.astype(BF16)
            slot = jnp.where(core == h, apart - 1, apart + 3)

            @pl.when((apart != 0) | (core != h))
            def _(h=h, slot=slot):
                pltpu.make_async_remote_copy(
                    hsend.at[way, index, h], hgot.at[slot, unit], rs_send, rs_recv,
                    device_id=(group, f - core + h), device_id_type=MESH).start()

            @pl.when((apart == 0) & (core == h))
            def _(half=half):
                hown[unit] = half

    rings = {}
    for step, i in [(step, i) for step in range(5) for i in range(4)]:
        for flow in range(4):
            if step == 0 and flow % 2 == 0:
                block_wait(flow // 2, i)
            if (flow, i, step - 1) in rings:
                rings[flow, i, step - 1].wait_recv()
            if step < 3 or step == 3 and (i < 2) == (flow % 2 == 0):
                rings[flow, i, step] = ring_copy(flow, i, step)
                rings[flow, i, step].start()
        if i < 3:
            continue
        for shift in (-step, step) if 0 < step < 4 else (step,):
            send_partial(0, z + shift)
            send_partial(1, x + shift)

    for copy in hid_copies:
        copy.wait_recv()
    for n in range(COLS // 256):
        part = slice(n * 256, (n + 1) * 256)
        total = None
        for group in range(N_DP):
            term = jnp.dot(hid[group], cot[group, :, :, :, part].reshape(TOK, 256), preferred_element_type=F32)
            total = term if total is None else total + term
        wout[0, :, part] = total[:FF]
        wout[1, :, part] = total[PAD:PAD + FF]

    weights, ggrads, ugrads = (a_w, c_w), (a_g, c_g), (a_u, c_u)

    def weight_copies(m):
        return (
            pltpu.make_async_copy(wout.at[0], weights[m], out_sem.at[0]),
            pltpu.make_async_remote_copy(
                wout.at[1], weights[m], out_send, out_recv, device_id=sib, device_id_type=MESH),
        )

    by_core(lambda m: [copy.start() for copy in weight_copies(m)])

    pltpu.make_async_copy(hgot, hgot, rs_recv).wait()
    perm = permutation(k)
    for i, slots in enumerate(((0, 1, 2), (3, 4, 5, 6))):
        grad = hown[...] if i == 0 else 0.0
        for slot in slots:
            grad = grad + hgot[slot].astype(F32)
        grad = grad.reshape(TOK, 128)
        model = core if i == 0 else 1 - core
        for factor, out in ((gate_f, gout), (up_f, uout)):
            back = lax.dot_general(
                (grad * factor[model]).astype(BF16), perm, (((0,), (1,)), ((), ())), preferred_element_type=F32)
            out[i] = back[:FF].astype(BF16)

    def small_copies(m):
        return [
            pltpu.make_async_copy(src.at[i], outs[m if i == 0 else 1 - m], out_sem.at[1 + 2 * j + i])
            for i in range(2) for j, (src, outs) in enumerate(((gout, ggrads), (uout, ugrads)))
        ]

    by_core(lambda m: [copy.start() for copy in small_copies(m)])

    pl.when(jnp.logical_not(own_p0))(stage0.pop().wait_send)
    for copy in stage0 + stage1 + hid_copies + list(rings.values()):
        copy.wait_send()
    pltpu.make_async_copy(hgot, hgot, rs_send).wait()

    def finish(m):
        for copy in small_copies(m):
            copy.wait()
        local, remote = weight_copies(m)
        local.wait()
        remote.wait_send()
        pltpu.make_async_remote_copy(
            wout.at[1], weights[1 - m], out_send, out_recv, device_id=sib, device_id_type=MESH).wait_recv()

    by_core(finish)


def store(*refs):
    ins, outs, held, (in_sem, out_sem) = refs[:6], refs[6:12], refs[12:18], refs[18:]
    loads = [pltpu.make_async_copy(ins[i], held[i], in_sem.at[i]) for i in range(6)]
    stores = [pltpu.make_async_copy(held[i], outs[i], out_sem.at[i]) for i in range(6)]
    for copy in loads:
        copy.start()
    for load, copy in zip(loads, stores):
        load.wait()
        copy.start()
    for copy in stores:
        copy.wait()


def on_device(*args):
    hbm_spec = pl.BlockSpec(memory_space=pltpu.HBM)
    dma, vmem = pltpu.SemaphoreType.DMA, pltpu.VMEM
    weight = jax.ShapeDtypeStruct((FF, COLS), F32)
    small = jax.ShapeDtypeStruct((FF, TOK), BF16)
    results = pl.pallas_call(
        kernel,
        out_shape=(weight, small, small, weight, small, small),
        in_specs=[hbm_spec] * 8,
        out_specs=(hbm_spec,) * 6,
        scratch_shapes=[
            vmem((2, 1, D), BF16),
            vmem((8, 1, COLS), F32),
            vmem((16, 1, COLS), F32),
            vmem((16, COLS), F32),
            vmem((2, FF, TOK), BF16),
            vmem((2, FF, TOK), BF16),
            vmem((FF, TOK), BF16),
            vmem((FF, TOK), BF16),
            vmem((2, FF, COLS), BF16),
            vmem((256, COLS), BF16),
            vmem((2, TOK, 128), F32),
            vmem((2, TOK, 128), F32),
            vmem((N_DP, ROWS, TOK), BF16),
            vmem((N_DP, 4, 4, 16, COLS), BF16),
            vmem((4, 4, 16, 128), F32),
            vmem((2, 8, 2, 4, 16, 128), BF16),
            vmem((7, 4, 4, 16, 128), BF16),
            vmem((2, FF, COLS), F32),
            vmem((2, FF, TOK), BF16),
            vmem((2, FF, TOK), BF16),
            dma((7,)),
            dma((3,)),
            dma((3,)),
            dma((16,)),
            dma,
            dma((7,)),
            dma((2, 4)),
            dma((4, 4, 4)),
            dma((4, 4, 4)),
            dma((3,)),
            dma((3,)),
            dma,
            dma,
            dma((5,)),
            dma,
            dma,
        ],
        compiler_params=pltpu.CompilerParams(
            collective_id=0, has_side_effects=True, vmem_limit_bytes=VMEM_LIMIT),
        cost_estimate=pl.CostEstimate(flops=1_200_000_000, bytes_accessed=4_000_000, transcendentals=200_000),
        name="mlp_backward",
    )(*args)
    return pl.pallas_call(
        store,
        out_shape=(weight, small, small, weight, small, small),
        in_specs=[hbm_spec] * 6,
        out_specs=(hbm_spec,) * 6,
        scratch_shapes=[vmem(a.shape, a.dtype) for a in results] + [dma((6,)), dma((6,))],
        compiler_params=pltpu.CompilerParams(vmem_limit_bytes=VMEM_LIMIT),
        name="store_results",
    )(*results)


def solution(mesh):
    placed = (
        P("fsdp", "dp"),
        P("fsdp", "dp"),
        P(("dp", "fsdp"), None),
        P("fsdp", None),
    )
    return jax.shard_map(
        on_device,
        mesh=mesh,
        in_specs=placed * 2,
        out_specs=(P("fsdp", "dp"),) * 6,
        check_vma=False,
    )
```

time: 66.5 us -> 63.7 us (0.958)
  Pallas kernels: 65.7 us -> 62.9 us
    pallas_call x1, Pallas kernels: 63.5 us -> 60.7 us  [on_device(): pl.pallas_call(kernel, out_shape=(weight, small, small, weight, small, sm...]
where the time goes in v3:
time: 63.7 us; the launch traced here: 63.5 us
  Pallas kernels  62.9 us (99%)
  between operations  0.64 us (1%)
    pallas_call x1, Pallas kernels, on_device(): pl.pallas_call(kernel, out_shape=(weight, small, small, weight, small, sm...  60.7 us
    pallas_call x1, Pallas kernels, on_device(): pl.pallas_call(store, out_shape=(weight, small, small, weight, small, sma...  2.22 us

profile of v3, /device:TPU:1, one launch (start us, length us, event | category | flops | bytes accessed | tf_op | source)
XLA Modules:
  0.0 63.5 jit_solution(1717559073053985555)
XLA Ops:
  0.6 60.7 %mlp_backward.1 = (f32[108,1280]{1,0:T(8,128)}, bf16[108,256]{1,0:T(8,128)(2,1)}, bf16[108,256]{1,0:T(8,128)(2,1)}, f32[108,1280]{1,0:T(8,128)}, bf16[108,256]{1,0:T(8,128)(2,1)}, /*index=5*/bf16[108,256]{1,0:T(8,128)(2,1)}) custom-call(bf16[108,256]{1,0:T(8,128)(2,1)} %a_gate.1, bf16[108,256]{1,0:T(8,128)(2,1)} %a_up.1, bf16[1,5120]{1,0:T(2,128)(2,1)} %a_cot.1, ...), custom_call_target="tpu_custom_call" | custom-call | flops 1200000000 | bytes 4000000 | tf_op jit(solution)/shard_map/mlp_backward/pallas_call | solution.py:341
  61.3 2.2 %store_results.1 = (f32[108,1280]{1,0:T(8,128)}, bf16[108,256]{1,0:T(8,128)(2,1)}, bf16[108,256]{1,0:T(8,128)(2,1)}, f32[108,1280]{1,0:T(8,128)}, bf16[108,256]{1,0:T(8,128)(2,1)}, /*index=5*/bf16[108,256]{1,0:T(8,128)(2,1)}) custom-call(f32[108,1280]{1,0:T(8,128)} %get-tuple-element.12.refs_0_, bf16[108,256]{1,0:T(8,128)(2,1)} %get-tuple-element.13.refs_1_, ...), custom_call_target="tpu_custom_call" | custom-call | tf_op jit(solution)/shard_map/store_results/pallas_call | solution.py:389
